TPU v7x, 256 devices: a whole 4x4x8 slice. The times are simulated.
256 devices in a mesh: rows: 64 (over z, y, core), rel: 4 (over x).
Axes of the slice: x: 4, y: 4, z: 8, core: 2. Of those that a mesh axis runs over, the one named last changes fastest.
Arguments:
- entities: float32 [131072, 400], P('rows'), may hold values from -0.6 to 0.6
- entity_state: float32 [131072], P('rows'), may hold values from 0.02 to 0.5
- relations: float32 [8, 400, 400], P('rel'), may hold values from -1.5 to 1.5
- relation_state: float32 [8, 400, 400], P('rel'), may hold values from 1 to 100
- head_block: int32 [131072, 1], P(('rows', 'rel')), may hold values from 0 to 63; in each aligned block of 512 rows (0 to 511, 512 to 1023, ...) at most 24 rows name the same one
- head_row: int32 [131072], P(('rows', 'rel')), may hold values from 0 to 2047
- tail_block: int32 [131072, 1], P(('rows', 'rel')), may hold values from 0 to 63; in each aligned block of 512 rows (0 to 511, 512 to 1023, ...) at most 24 rows name the same one
- tail_row: int32 [131072], P(('rows', 'rel')), may hold values from 0 to 2047
- rel_slot: int32 [131072], P(('rows', 'rel')), may hold values from 0 to 1
- neg_block: int32 [131072, 1], P(('rows', 'rel')), may hold values from 0 to 63; in each aligned block of 512 rows (0 to 511, 512 to 1023, ...) at most 24 rows name the same one
- neg_row: int32 [131072], P(('rows', 'rel')), may hold values from 0 to 2047
Outputs:
- new_entities: float32 [131072, 400], P('rows')
- new_entity_state: float32 [131072], P('rows')
- new_relations: float32 [8, 400, 400], P('rel')
- new_relation_state: float32 [8, 400, 400], P('rel')
Inputs may be any that keep to these rules, and one draw needn't show every extreme that they name: `head_block`: among the edges of one device, no row block holds more than 24 heads; some row block holds exactly 24. `tail_block`: among the edges of one device, no row block holds more than 24 tails; some row block holds exactly 24. `neg_block`: among the negatives of one group, no row block holds more than 24; some row block holds exactly 24.
All inputs are finite; a program needn't handle non-finite values.
Results may differ from a plain program's by a relative error of at most 0.0003.
Values sent between devices are 32-bit elements; how exact they have to be, the bound alone decides.
A program may use at most 128 MiB of HBM per device.

v0:
```python
import jax
import jax.numpy as jnp
from jax import lax
from jax.sharding import PartitionSpec as P

highest = lax.Precision.HIGHEST
entity_rate = 0.1
relation_rate = 0.1


def edge_grads(head_vecs, tail_vecs, neg_vecs, rel_pair, slot_ids):
    choices_count = rel_pair.shape[0]
    member = (slot_ids[:, None] == jnp.arange(choices_count, dtype=jnp.int32)[None, :]).astype(
        jnp.float32
    )
    products = jnp.einsum("ed,kdf->kef", head_vecs, rel_pair, precision=highest)
    projected = jnp.einsum("ek,kef->ef", member, products, precision=highest)
    pos_score = jnp.sum(projected * tail_vecs, axis=-1)
    neg_score = jnp.dot(projected, neg_vecs.T, precision=highest)
    pos_weight = -jax.nn.sigmoid(-pos_score)
    neg_weight = jax.nn.sigmoid(neg_score) / neg_vecs.shape[0]
    proj_grad = pos_weight[:, None] * tail_vecs + jnp.dot(neg_weight, neg_vecs, precision=highest)
    backward = jnp.einsum("ef,kdf->ked", proj_grad, rel_pair, precision=highest)
    head_grad = jnp.einsum("ek,ked->ed", member, backward, precision=highest)
    tail_grad = pos_weight[:, None] * projected
    neg_grad = jnp.dot(neg_weight.T, projected, precision=highest)
    rel_grad = jnp.einsum("ed,ek,ef->kdf", head_vecs, member, proj_grad, precision=highest)
    return (head_grad, tail_grad, neg_grad, rel_grad)


def place_slots(blocks, owners, slot_width, offset):
    member = (blocks[:, None] == jnp.arange(owners, dtype=jnp.int32)[None, :]).astype(jnp.int32)
    earlier = jnp.cumsum(member, axis=0) - member
    position = jnp.sum(earlier * member, axis=1)
    return blocks * slot_width + offset + position


def adagrad_rows(row_block, accum, gradient):
    updated = accum + jnp.mean(gradient * gradient, axis=1)
    return (row_block - entity_rate * gradient / jnp.sqrt(updated)[:, None], updated)


def adagrad_dense(params, accum, gradient):
    updated = accum + gradient * gradient
    return (params - relation_rate * gradient / jnp.sqrt(updated), updated)


def per_device(
    entities,
    entity_state,
    relations,
    relation_state,
    head_block,
    head_row,
    tail_block,
    tail_row,
    rel_slot,
    neg_block,
    neg_row,
):
    owners = lax.axis_size("rows")
    edge_count = head_row.shape[0]
    neg_count = neg_row.shape[0]
    local_rows = entities.shape[0]
    cap_edges = 3 * edge_count // owners
    cap_negs = 3 * neg_count // owners
    slot_width = 2 * cap_edges + cap_negs
    head_slot = place_slots(head_block[:, 0], owners, slot_width, 0)
    tail_slot = place_slots(tail_block[:, 0], owners, slot_width, cap_edges)
    neg_slot = place_slots(neg_block[:, 0], owners, slot_width, 2 * cap_edges)
    wanted = jnp.full((owners * slot_width,), local_rows, jnp.int32)
    wanted = (
        wanted.at[head_slot].set(head_row).at[tail_slot].set(tail_row).at[neg_slot].set(neg_row)
    )
    requested = lax.all_to_all(
        wanted.reshape(owners, slot_width), "rows", split_axis=0, concat_axis=0, tiled=True
    )
    answered = jnp.take(entities, requested, axis=0, mode="fill", fill_value=0.0)
    fetched = lax.all_to_all(answered, "rows", split_axis=0, concat_axis=0, tiled=True).reshape(
        owners * slot_width, -1
    )
    head_grad, tail_grad, neg_grad, rel_grad = edge_grads(
        fetched[head_slot], fetched[tail_slot], fetched[neg_slot], relations, rel_slot
    )
    outgoing = (
        jnp.zeros_like(fetched)
        .at[head_slot]
        .set(head_grad)
        .at[tail_slot]
        .set(tail_grad)
        .at[neg_slot]
        .set(neg_grad)
    )
    returned = lax.all_to_all(
        outgoing.reshape(owners, slot_width, -1), "rows", split_axis=0, concat_axis=0, tiled=True
    )
    partial_grad = (
        jnp.zeros_like(entities)
        .at[requested.reshape(-1)]
        .add(returned.reshape(owners * slot_width, -1), mode="drop")
    )
    summed = lax.psum(partial_grad, "rel")
    new_entities, new_entity_state = adagrad_rows(entities, entity_state, summed)
    rel_summed = lax.psum(rel_grad, "rows")
    new_relations, new_relation_state = adagrad_dense(relations, relation_state, rel_summed)
    return (new_entities, new_entity_state, new_relations, new_relation_state)


def solution(mesh):
    placed = (
        P("rows", None),
        P("rows"),
        P("rel", None, None),
        P("rel", None, None),
        P(("rows", "rel"), None),
        P(("rows", "rel")),
        P(("rows", "rel"), None),
        P(("rows", "rel")),
        P(("rows", "rel")),
        P(("rows", "rel"), None),
        P(("rows", "rel")),
    )
    return jax.shard_map(
        per_device,
        mesh=mesh,
        in_specs=placed,
        out_specs=(P("rows", None), P("rows"), P("rel", None, None), P("rel", None, None)),
        check_vma=False,
    )
```

profile of v0, /device:TPU:1, one launch (start us, length us, event | category | flops | bytes accessed | tf_op | source)
XLA Modules:
  0.0 762.6 jit_solution(14571085221006425935)
XLA Ops:
  7.2 0.7 fusion.23
  7.9 1.2 reduce-window.20
  9.4 0.8 fusion.22
  10.9 0.7 fusion.24
  11.6 1.2 reduce-window.24
  13.0 0.8 fusion.19
  15.2 1.2 reduce-window.26
  16.7 0.8 fusion.16
  18.2 2.6 scatter_custom_fusion
  20.8 2.8 scatter_fusion
  23.6 2.5 scatter_fusion.1
  26.1 0.7 all_to_all.16
  26.9 13.2 %all-to-all-start = ((s32[64,1,72]{2,1,0:T(1,128)}), s32[64,1,72]{2,1,0:T(1,128)S(1)}, u32[]{:S(2)}, u32[]{:S(2)}) async-start(s32[64,1,72]{2,1,0:T(1,128)} %all_to_all.16), calls=%async_computation | async-start | bytes 65536 | tf_op jit(solution)/shard_map/all_to_all | solution.py:75
  40.1 3.4 copy.40
  43.4 5.9 all-to-all-done
  49.5 17.0 %gather_fusion = f32[4608,400]{1,0:T(8,128)} fusion(f32[2048,400]{1,0:T(8,128)} %copy.40, s32[5120]{0:T(1024)S(1)} %pad_clamp_fusion), kind=kCustom, calls=%fused_computation | custom fusion | bytes 14764032 | tf_op jit(solution)/shard_map/jit(_take)/gather | solution.py:78
  66.5 8.6 %broadcast_select_fusion = f32[64,72,400]{2,1,0:T(8,128)} fusion(f32[64,72,400]{2,1,0:T(8,128)} %bitcast.99, pred[64,72]{1,0:T(8,128)(4,1)S(1)} %compare_and_fusion), kind=kLoop, calls=%fused_computation.11 | loop fusion | flops 1843200 | bytes 14750208 | tf_op jit(solution)/shard_map/jit(_take)/select_n | solution.py:78
  75.1 6.6 all-to-all-start.1
  81.7 204.5 %all-to-all-done.1 = f32[64,72,400]{2,1,0:T(8,128)} async-done(((f32[64,72,400]{2,1,0:T(8,128)}), f32[64,72,400]{2,1,0:T(8,128)}, u32[]{:S(2)}, u32[]{:S(2)}) %all-to-all-start.1) | async-done | bytes 7372832 | tf_op jit(solution)/shard_map/all_to_all | solution.py:79
  286.2 5.7 gather_fusion.1
  291.9 6.5 gather_fusion.3
  298.4 3.6 multiply_reduce_fusion.2
  302.0 4.8 fusion.9
  306.8 1.0 copy-done.2
  307.8 4.4 fusion.30
  312.2 6.6 gather_fusion.2
  318.8 2.4 copy.36
  321.2 1.3 multiply_reduce_fusion.3
  322.5 1.0 broadcast_multiply_fusion
  323.5 3.9 fusion.10
  327.4 2.5 copy.38
  329.8 3.7 multiply_reduce_fusion.1
  333.5 2.5 copy.55
  335.9 7.1 scatter_custom_fusion.3
  343.1 10.2 %scatter_fusion.2 = f32[4608,400]{1,0:T(8,128)} fusion(f32[4608,400]{1,0:T(8,128)} %scatter_custom_fusion.3, s32[512]{0:T(512)S(1)} %bitcast.104, f32[512,400]{1,0:T(8,128)} %copy.38), kind=kCustom, calls=%fused_computation.8 | custom fusion | bytes 2459648 | tf_op jit(solution)/shard_map/scatter | solution.py:90
  353.3 10.4 %scatter_fusion.3 = f32[4608,400]{1,0:T(8,128)} fusion(f32[4608,400]{1,0:T(8,128)} %scatter_fusion.2, s32[512]{0:T(512)S(1)} %bitcast.107, f32[512,400]{1,0:T(8,128)} %fusion.30), kind=kCustom, calls=%fused_computation.9 | custom fusion | bytes 2459648 | tf_op jit(solution)/shard_map/scatter | solution.py:92
  363.7 11.3 %all-to-all-start.2 = ((f32[64,72,400]{2,1,0:T(8,128)}), f32[64,72,400]{2,1,0:T(8,128)}, u32[]{:S(2)}, u32[]{:S(2)}) async-start(f32[64,72,400]{2,1,0:T(8,128)} %bitcast.98), calls=%async_computation.2 | async-start | bytes 18874368 | tf_op jit(solution)/shard_map/all_to_all | solution.py:94
  375.1 1.2 copy.41
  376.3 5.0 fusion.4
  381.9 0.7 reduce.15
  382.8 205.8 %all-to-all-done.2 = f32[64,72,400]{2,1,0:T(8,128)} async-done(((f32[64,72,400]{2,1,0:T(8,128)}), f32[64,72,400]{2,1,0:T(8,128)}, u32[]{:S(2)}, u32[]{:S(2)}) %all-to-all-start.2) | async-done | bytes 7372832 | tf_op jit(solution)/shard_map/all_to_all | solution.py:94
  588.6 30.6 %scatter_custom_fusion.6 = f32[2048,400]{1,0:T(8,128)} fusion(s32[4608]{0:T(1024)S(1)} %fusion.26, f32[4608,400]{1,0:T(8,128)} %bitcast.28, f32[]{:T(128)} %constant.15.clone.1), kind=kCustom, calls=%fused_computation.16 | custom fusion | flops 1843200 | bytes 3277312 | tf_op jit(solution)/shard_map/scatter-add | solution.py:100
  619.3 23.0 %all-reduce.5.cloned.1.call-done = f32[2,400,400]{2,1,0:T(8,128)} async-done(((f32[2,400,400]{2,1,0:T(8,128)}), f32[2,400,400]{2,1,0:T(8,128)}) %all-reduce.5.cloned.1.call-update) | async-done | bytes 1280016 | tf_op jit(solution)/shard_map/psum | solution.py:104
  642.3 3.8 multiply_subtract_fusion
  646.0 96.0 %all-reduce.3.cloned.1.call-done = f32[2048,400]{1,0:T(8,128)} async-done(((f32[2048,400]{1,0:T(8,128)}), f32[2048,400]{1,0:T(8,128)}) %all-reduce.3.cloned.1.call-update) | async-done | bytes 3276816 | tf_op jit(solution)/shard_map/psum | solution.py:102
  742.0 2.7 multiply_reduce_fusion
  745.5 4.9 divide_subtract_fusion
  750.3 5.2 copy.42
  (47 shorter events, 5.3 us)
Async XLA Ops:
  7.2 16.5 %copy-start.7 = (s32[512]{0:T(512)S(1)}, s32[512]{0:T(512)}, u32[]{:S(2)}) copy-start(s32[512]{0:T(512)} %param.21) | copy-start | bytes 6148
  10.9 70.8 %copy-start.5 = (s32[512,1]{0,1:T(1,128)}, s32[512,1]{0,1:T(1,128)S(1)}, u32[]{:S(2)}) copy-start(s32[512,1]{0,1:T(1,128)S(1)} %compare_select_fusion.5) | copy-start | bytes 6148
  20.8 19.2 %copy-start.3 = (f32[2048,400]{0,1:T(8,128)S(1)}, f32[2048,400]{0,1:T(8,128)}, u32[]{:S(2)}) copy-start(f32[2048,400]{0,1:T(8,128)} %param.11) | copy-start | bytes 9830404
  26.9 22.5 %all-to-all-start = ((s32[64,1,72]{2,1,0:T(1,128)}), s32[64,1,72]{2,1,0:T(1,128)S(1)}, u32[]{:S(2)}, u32[]{:S(2)}) async-start(s32[64,1,72]{2,1,0:T(1,128)} %all_to_all.16), calls=%async_computation | async-start | bytes 65536 | tf_op jit(solution)/shard_map/all_to_all | solution.py:75
  75.1 6.6 copy-start.8
  75.1 211.1 %all-to-all-start.1 = ((f32[64,72,400]{2,1,0:T(8,128)}), f32[64,72,400]{2,1,0:T(8,128)}, u32[]{:S(2)}, u32[]{:S(2)}) async-start(f32[64,72,400]{2,1,0:T(8,128)} %broadcast_select_fusion), calls=%async_computation.1 | async-start | bytes 18874368 | tf_op jit(solution)/shard_map/all_to_all | solution.py:79
  291.9 6.5 copy-start.1
  306.8 1.0 copy-start.2
  363.7 224.9 %all-to-all-start.2 = ((f32[64,72,400]{2,1,0:T(8,128)}), f32[64,72,400]{2,1,0:T(8,128)}, u32[]{:S(2)}, u32[]{:S(2)}) async-start(f32[64,72,400]{2,1,0:T(8,128)} %bitcast.98), calls=%async_computation.2 | async-start | bytes 18874368 | tf_op jit(solution)/shard_map/all_to_all | solution.py:94
  375.0 267.2 %all-reduce.5.cloned.1.call-start = ((), (), s32[]{:S(2)}) async-start(), calls=%async_computation.4 | async-start | bytes 3276800 | tf_op jit(solution)/shard_map/psum | solution.py:104
  381.3 360.7 %all-reduce.3.cloned.1.call-start = ((), (), s32[]{:S(2)}) async-start(), calls=%async_computation.3 | async-start | bytes 8388608 | tf_op jit(solution)/shard_map/psum | solution.py:102
  588.6 53.6 %copy-start.4 = (f32[2,400,400]{2,1,0:T(8,128)S(1)}, f32[2,400,400]{2,1,0:T(8,128)}, u32[]{:S(2)}) copy-start(f32[2,400,400]{2,1,0:T(8,128)} %param.14) | copy-start | bytes 3840004
  619.2 125.5 %copy-start.6 = (f32[2048]{0:T(1024)S(1)}, f32[2048]{0:T(1024)}, u32[]{:S(2)}) copy-start(f32[2048]{0:T(1024)} %param.12) | copy-start | bytes 24580
  742.0 3.4 copy-start
Sparse Core Ops, SparseCore 0:
  381.5 260.7 all-reduce.4
  644.6 97.3 all-reduce.2
where the time goes:
time: 770 us; the launch traced here: 763 us
  waiting for transfers between devices  535 us (69%)
  local copies, waits for them, and re-layouts  91.7 us (12%)
  other arithmetic  64.6 us (8%)
  starting transfers between devices  31.1 us (4%)
  matrix products  25.4 us (3%)
  between operations  14.5 us (2%)
    all_to_all x1, waiting for transfers between devices, per_device(): lax.all_to_all(outgoing.reshape(owners, slot_width, -1), 'rows', split_ax...  206 us
    all_to_all x1, waiting for transfers between devices, per_device(): lax.all_to_all(answered, 'rows', split_axis=0, concat_axis=0, tiled=True)  204 us
    psum x1, waiting for transfers between devices, per_device(): summed = lax.psum(partial_grad, 'rel')  96 us
    scatter-add x1, other arithmetic, per_device(): partial_grad = jnp.zeros_like(entities).at[requested.reshape(-1)].add(ret...  30.6 us
    scatter x3, local copies, waits for them, and re-layouts, per_device(): outgoing = jnp.zeros_like(fetched).at[head_slot].set(head_grad).at[tail_s...  27.7 us
    psum x1, waiting for transfers between devices, per_device(): rel_summed = lax.psum(rel_grad, 'rows')  23 us
    gather x1, local copies, waits for them, and re-layouts, per_device(): jnp.take(entities, requested, axis=0, mode='fill', fill_value=0.0)  17 us
  transfers between devices with their start and end apart: 5, of which 5 were waited for; matrix products, arithmetic and copies ran while one was open for 6% of the time, Pallas kernels for 0%

commit v1 on v0

v1 whole, which is shorter than its diff:
```python
import functools

import jax
import jax.numpy as jnp
from jax import lax
from jax.experimental import pallas as pl
from jax.experimental.pallas import tpu as pltpu
from jax.sharding import PartitionSpec as P

MESH = pl.DeviceIdType.MESH
entity_rate = 0.1
relation_rate = 0.1
LANES = 128
NZ = 8
VMEM_LIMIT = 56 * 2**20
f32, bf16 = jnp.float32, jnp.bfloat16


def split(x):
    hi = x.astype(bf16)
    return hi, (x - hi.astype(f32)).astype(bf16)


def mm(a, b, dims=((1,), (0,))):
    return lax.dot_general(a, b, (dims, ((), ())), preferred_element_type=f32)


def mm3(a, b, dims=((1,), (0,))):
    ah, al = a
    bh, bl = b
    return mm(ah, bh, dims) + (mm(ah, bl, dims) + mm(al, bh, dims))


def iota(shape, axis):
    return lax.broadcasted_iota(jnp.int32, shape, axis)


def as_column(row, n):
    return jnp.sum(
        jnp.where(iota((n, n), 0) == iota((n, n), 1), jnp.broadcast_to(row, (n, n)), 0.0),
        axis=1,
        keepdims=True,
    )


def as_row(column, n):
    return jnp.sum(
        jnp.where(iota((n, n), 0) == iota((n, n), 1), jnp.broadcast_to(column, (n, n)), 0.0),
        axis=0,
        keepdims=True,
    )


def route_kernel(cap, hb, tb, nb, rows, want_ref, slot_ref):
    n = hb.shape[0]
    owners = want_ref.shape[0]
    before = (iota((n, n), 1) < iota((n, n), 0)).astype(bf16)
    lists = jnp.zeros((owners, LANES), f32)
    slots = jnp.zeros((n, LANES), f32)
    lane = iota((n, LANES), 1).astype(f32)
    for s, ref in enumerate((hb, tb, nb)):
        block = ref[...].astype(f32)
        member = lane == block
        earlier = mm(before, member.astype(bf16))
        pos = jnp.sum(jnp.where(member, earlier, 0.0), axis=1, keepdims=True)
        slots = jnp.where(lane == s, block * cap + pos, slots)
        value = as_column(rows[s : s + 1, :].astype(f32), n) + 1.0
        high = jnp.floor(value * (1.0 / 64.0))
        low = value - 64.0 * high
        at = lane == pos + float(cap * s)
        to_owner = (iota((owners, n), 0).astype(f32) == as_row(block, n)).astype(bf16)
        lists = (
            lists
            + 64.0 * mm(to_owner, jnp.where(at, high, 0.0).astype(bf16))
            + mm(to_owner, jnp.where(at, low, 0.0).astype(bf16))
        )
    slots = jnp.where(lane == 3, as_column(rows[3:4, :].astype(f32), n), slots)
    want_ref[...] = jnp.broadcast_to((lists - 1.0)[:, None, :], want_ref.shape)
    slot_ref[...] = slots


def partner(b, j, sign, nyc):
    me = lax.axis_index("rows")
    z, yc = me // nyc, me % nyc
    dz = (j + 1) // 2 if j % 2 else (NZ - j // 2) % NZ
    if sign > 0:
        return ((z + dz) % NZ) * nyc + (yc + b + j) % nyc
    return ((z + NZ - dz) % NZ) * nyc + (yc + 2 * nyc - b - j % nyc) % nyc


def meet_all(nyc):
    barrier = pltpu.get_barrier_semaphore()

    def greet(b, carry):
        for j in range(NZ):
            p = partner(b, j, 1, nyc)

            def tell():
                pl.semaphore_signal(barrier, inc=1, device_id={"rows": p}, device_id_type=MESH)

            if j == 0:
                pl.when(b > 0)(tell)
            else:
                tell()
        return carry

    lax.fori_loop(0, nyc, greet, 0)
    pl.semaphore_wait(barrier, NZ * nyc - 1)


def for_others(nyc, sign, body):
    def step(b, carry):
        for j in range(NZ):
            p = partner(b, j, sign, nyc)
            if j == 0:
                pl.when(b > 0)(functools.partial(body, p))
            else:
                body(p)
        return carry

    lax.fori_loop(0, nyc, step, 0)


def remote(src, dst, send, recv, p):
    return pltpu.make_async_remote_copy(
        src_ref=src, dst_ref=dst, send_sem=send, recv_sem=recv, device_id={"rows": p}, device_id_type=MESH
    )


def fetch_kernel(
    want, ent, fetched, asked, hi, lo, stage, isend, irecv, send, recv
):
    me = lax.axis_index("rows")
    owners = want.shape[0]
    nyc = owners // NZ
    rows, width = ent.shape
    full = width // LANES * LANES
    slots = 72
    meet_all(nyc)

    def index_copy(p, slot):
        return remote(want.at[p], asked.at[slot], isend.at[p], irecv.at[slot], p)

    for_others(nyc, 1, lambda p: index_copy(p, me).start())
    asked[me] = want[me]

    def cut(i, carry):
        at = pl.ds(pl.multiple_of(i * 256, 256), 256)
        h, l = split(ent[at, :full])
        hi[at, :full] = h
        lo[at, :full] = l
        hi[at, full:] = jnp.zeros((256, LANES), bf16)
        lo[at, full:] = jnp.zeros((256, LANES), bf16)
        h, l = split(ent[at, full:])
        hi[at, full:width] = h
        lo[at, full:width] = l
        return carry

    lax.fori_loop(0, rows // 256, cut, 0)
    for_others(nyc, 1, lambda p: index_copy(p, p).wait_recv())
    chunk = 512

    def answer(b, carry):
        to = [partner(b, j, 1, nyc) for j in range(NZ)]
        ids = jnp.concatenate([as_column(asked[p][0:1, :], LANES)[:slots] for p in to], axis=0)
        ids = ids.astype(jnp.int32)

        def gather(c, total):
            at = pl.ds(pl.multiple_of(c * chunk, chunk), chunk)
            pick = (ids - c * chunk == iota((NZ * slots, chunk), 1)).astype(bf16)
            return total + (mm(pick, hi[at, :]) + mm(pick, lo[at, :]))

        found = lax.fori_loop(
            0, rows // chunk, gather, jnp.zeros((NZ * slots, full + LANES), f32)
        )
        for j, p in enumerate(to):
            pack(stage, p, found[j * slots : (j + 1) * slots])
            copy = remote(stage.at[p], fetched.at[me], send.at[p], recv.at[me], p)
            if j == 0:
                pl.when(b > 0)(copy.start)
            else:
                copy.start()
        return carry

    lax.fori_loop(0, nyc, answer, 0)
    fetched[me] = stage[me]

    def finish(p):
        index_copy(p, p).wait_send()
        copy = remote(stage.at[p], fetched.at[p], send.at[p], recv.at[p], p)
        copy.wait_send()
        copy.wait_recv()

    for_others(nyc, 1, finish)


def pack(ref, p, block):
    slots = block.shape[0]
    planes = block.shape[1] // LANES - 1
    for c in range(planes):
        ref[p, c * slots : (c + 1) * slots, :] = block[:, c * LANES : (c + 1) * LANES]
    tail = block[:, planes * LANES :]
    packed = tail[0:8]
    for g in range(1, 8):
        packed = packed + pltpu.roll(tail[8 * g : 8 * g + 8], 16 * g, 1)
    ref[p, planes * slots : planes * slots + 8, :] = packed
    ref[p, planes * slots + 8 : planes * slots + 16, :] = tail[64:72]


def unpack_tail(ref, p, base):
    packed = ref[p, base : base + 8, :]
    low = iota((8, LANES), 1) < 16
    parts = [jnp.where(low, packed, 0.0)]
    for g in range(1, 8):
        parts.append(jnp.where(low, pltpu.roll(packed, LANES - 16 * g, 1), 0.0))
    parts.append(ref[p, base + 8 : base + 16, :])
    return jnp.concatenate(parts, axis=0)


def edge_kernel(
    fetched, rel, slots, out, rel_grad, xh, xl, vecs, grads, whole, rh, rl
):
    owners = fetched.shape[0]
    edges = slots.shape[0]
    width = rel.shape[1]
    full = width // LANES * LANES
    wide = full + LANES
    cap = 3 * edges // owners
    per = 3 * cap
    base = full // LANES * per
    total = owners * cap
    step = min(256, edges)
    low8 = iota((8, LANES), 1) < 16

    rh[...] = jnp.zeros(rh.shape, bf16)
    rl[...] = jnp.zeros(rl.shape, bf16)
    for k in range(rel.shape[0]):
        h, l = split(rel[k])
        rh[k, :width, :width] = h
        rl[k, :width, :width] = l

    for s in range(3):

        def collect(i, carry, s=s):
            at = pl.ds(pl.multiple_of(i * 8 * cap, 8 * cap), 8 * cap)
            from_ = pl.ds(i * 8, 8)
            for c in range(full // LANES):
                v = fetched[from_, c * per + s * cap : c * per + (s + 1) * cap, :]
                h, l = split(v.reshape(8 * cap, LANES))
                xh[at, c * LANES : (c + 1) * LANES] = h
                xl[at, c * LANES : (c + 1) * LANES] = l
            packed = fetched[from_, base : base + 8, :].reshape(64, LANES)
            low = iota((64, LANES), 1) < 16
            parts = []
            for g in range(3 * s, 3 * s + 3):
                if g == 8:
                    part = fetched[from_, base + 8 : base + 16, :].reshape(64, LANES)
                elif g == 0:
                    part = jnp.where(low, packed, 0.0)
                else:
                    part = jnp.where(low, pltpu.roll(packed, LANES - 16 * g, 1), 0.0)
                parts.append(part.reshape(8, 1, 8, LANES))
            h, l = split(jnp.concatenate(parts, axis=1).reshape(8 * cap, LANES))
            xh[at, full:] = h
            xl[at, full:] = l
            return carry

        lax.fori_loop(0, owners // 8, collect, 0)

        def choose(i, carry, s=s):
            at = pl.ds(pl.multiple_of(i * step, step), step)
            place = slots[at, :][:, s : s + 1].astype(jnp.int32)
            pick = (place == iota((step, total), 1)).astype(bf16)
            vecs[s, at, :] = mm(pick, xh[...]) + mm(pick, xl[...])
            return carry

        lax.fori_loop(0, edges // step, choose, 0)

    grads[2] = jnp.zeros((edges, wide), f32)
    whole[0:wide] = jnp.zeros((wide, wide), f32)
    whole[wide : 2 * wide] = jnp.zeros((wide, wide), f32)
    last = ((1,), (1,))

    def grad(i, carry):
        at = pl.ds(pl.multiple_of(i * step, step), step)
        head, tail = vecs[0, at, :], vecs[1, at, :]
        negs = split(vecs[2])
        second = slots[at, :][:, 3:4] > 0.5
        hs = split(head)
        r0, r1 = (rh[0], rl[0]), (rh[1], rl[1])
        projected = jnp.where(second, mm3(hs, r1), mm3(hs, r0))
        ps = split(projected)
        pos_score = jnp.sum(projected * tail, axis=1, keepdims=True)
        neg_score = mm3(ps, negs, last)
        pos_weight = -1.0 / (1.0 + jnp.exp(pos_score))
        neg_weight = (1.0 / (1.0 + jnp.exp(-neg_score))) * (1.0 / edges)
        proj_grad = pos_weight * tail + mm3(split(neg_weight), negs)
        gs = split(proj_grad)
        grads[0, at, :] = jnp.where(second, mm3(gs, r1, last), mm3(gs, r0, last))
        grads[1, at, :] = pos_weight * projected
        grads[2] = grads[2] + mm3(split(neg_weight.T), ps)
        ht = split(head.T)
        g1 = split(jnp.where(second, proj_grad, 0.0))
        g0 = split(jnp.where(second, 0.0, proj_grad))
        whole[0:wide] = whole[0:wide] + mm3(ht, g0)
        whole[wide : 2 * wide] = whole[wide : 2 * wide] + mm3(ht, g1)
        return carry

    lax.fori_loop(0, edges // step, grad, 0)
    rel_grad[0] = whole[0:width, 0:width]
    rel_grad[1] = whole[wide : wide + width, 0:width]

    for s in range(3):
        place = as_row(slots[:, s : s + 1], edges).astype(jnp.int32)
        gh, gl = split(grads[s])

        def spread(i, carry, s=s):
            at = i * 8 * cap
            put = (iota((8 * cap, edges), 0) + at == place).astype(bf16)
            v = mm(put, gh) + mm(put, gl)
            to = pl.ds(i * 8, 8)
            for c in range(full // LANES):
                out[to, c * per + s * cap : c * per + (s + 1) * cap, :] = v[
                    :, c * LANES : (c + 1) * LANES
                ].reshape(8, cap, LANES)
            tails = v[:, full:].reshape(8, 3, 8, LANES)
            packed = jnp.zeros((64, LANES), f32)
            for q in range(3):
                g = 3 * s + q
                part = tails[:, q].reshape(64, LANES)
                if g == 8:
                    out[to, base + 8 : base + 16, :] = part.reshape(8, 8, LANES)
                elif g == 0:
                    packed = packed + part
                else:
                    packed = packed + pltpu.roll(part, 16 * g, 1)
            packed = packed.reshape(8, 8, LANES)
            if s > 0:
                packed = packed + out[to, base : base + 8, :]
            out[to, base : base + 8, :] = packed
            return carry

        lax.fori_loop(0, owners // 8, spread, 0)


def return_kernel(msgs, asked, total, back, acc, xh, xl, send, recv):
    me = lax.axis_index("rows")
    owners = msgs.shape[0]
    nyc = owners // NZ
    rows, width = total.shape
    full = width // LANES * LANES
    slots = 72
    planes = full // LANES
    meet_all(nyc)

    def copy(p, slot):
        return remote(msgs.at[p], back.at[slot], send.at[p], recv.at[slot], p)

    for_others(nyc, 1, lambda p: copy(p, me).start())
    back[me] = msgs[me]
    xh[...] = jnp.zeros(xh.shape, bf16)
    xl[...] = jnp.zeros(xl.shape, bf16)

    def clear(i, carry):
        acc[pl.ds(pl.multiple_of(i * 256, 256), 256), :] = jnp.zeros((256, full + LANES), f32)
        return carry

    lax.fori_loop(0, rows // 256, clear, 0)

    def take(b, carry):
        origin = [partner(b, j, -1, nyc) for j in range(NZ)]
        for j, q in enumerate(origin):
            arrived = copy(q, q)
            if j == 0:
                pl.when(b > 0)(arrived.wait_recv)
            else:
                arrived.wait_recv()
            gap = jnp.zeros((8, LANES), f32)
            for c in range(planes + 1):
                if c < planes:
                    v = back[q, c * slots : (c + 1) * slots, :]
                else:
                    v = unpack_tail(back, q, planes * slots)
                h, l = split(jnp.concatenate([v, gap], axis=0))
                xh[j * LANES : j * LANES + 80, c * LANES : (c + 1) * LANES] = h
                xl[j * LANES : j * LANES + 80, c * LANES : (c + 1) * LANES] = l
        names = [asked[q][0:1, :].astype(jnp.int32) for q in origin]

        def add(m, inner):
            at = pl.ds(pl.multiple_of(m * 256, 256), 256)
            row = iota((256, LANES), 0) + m * 256
            put = jnp.concatenate([(row == name).astype(bf16) for name in names], axis=1)
            acc[at, :] = acc[at, :] + (mm(put, xh[...]) + mm(put, xl[...]))
            return inner

        lax.fori_loop(0, rows // 256, add, 0)
        return carry

    lax.fori_loop(0, nyc, take, 0)

    def store(i, carry):
        at = pl.ds(pl.multiple_of(i * 256, 256), 256)
        total[at, :] = acc[at, :][:, :width]
        return carry

    lax.fori_loop(0, rows // 256, store, 0)
    for_others(nyc, 1, lambda p: copy(p, p).wait_send())


def adagrad_rows(row_block, accum, gradient):
    updated = accum + jnp.mean(gradient * gradient, axis=1)
    return (row_block - entity_rate * gradient / jnp.sqrt(updated)[:, None], updated)


def adagrad_dense(params, accum, gradient):
    updated = accum + gradient * gradient
    return (params - relation_rate * gradient / jnp.sqrt(updated), updated)


def per_device(
    entities,
    entity_state,
    relations,
    relation_state,
    head_block,
    head_row,
    tail_block,
    tail_row,
    rel_slot,
    neg_block,
    neg_row,
):
    owners = lax.axis_size("rows")
    edges = head_row.shape[0]
    rows, width = entities.shape
    full = width // LANES * LANES
    wide = full + LANES
    cap = 3 * edges // owners
    message = full // LANES * 3 * cap + 16
    vmem = pl.BlockSpec(memory_space=pltpu.VMEM)
    shape = jax.ShapeDtypeStruct
    params = functools.partial(pltpu.CompilerParams, vmem_limit_bytes=VMEM_LIMIT)
    dma = pltpu.SemaphoreType.DMA((owners,))

    rows_in = jnp.stack([head_row, tail_row, neg_row, rel_slot])
    want, slots = pl.pallas_call(
        functools.partial(route_kernel, cap),
        out_shape=(shape((owners, 8, LANES), f32), shape((edges, LANES), f32)),
        in_specs=[vmem] * 4,
        out_specs=(vmem, vmem),
        compiler_params=params(),
        name="route",
    )(head_block, tail_block, neg_block, rows_in)

    fetched, asked = pl.pallas_call(
        fetch_kernel,
        out_shape=(shape((owners, message, LANES), f32), shape((owners, 8, LANES), f32)),
        in_specs=[vmem] * 2,
        out_specs=(vmem, vmem),
        scratch_shapes=[
            pltpu.VMEM((rows, wide), bf16),
            pltpu.VMEM((rows, wide), bf16),
            pltpu.VMEM((owners, message, LANES), f32),
            dma,
            dma,
            dma,
            dma,
        ],
        compiler_params=params(collective_id=0, has_side_effects=True),
        name="fetch",
    )(want, entities)

    out, rel_grad = pl.pallas_call(
        edge_kernel,
        out_shape=(shape((owners, message, LANES), f32), shape(relations.shape, f32)),
        in_specs=[vmem] * 3,
        out_specs=(vmem, vmem),
        scratch_shapes=[
            pltpu.VMEM((owners * cap, wide), bf16),
            pltpu.VMEM((owners * cap, wide), bf16),
            pltpu.VMEM((3, edges, wide), f32),
            pltpu.VMEM((3, edges, wide), f32),
            pltpu.VMEM((2 * wide, wide), f32),
            pltpu.VMEM((2, wide, wide), bf16),
            pltpu.VMEM((2, wide, wide), bf16),
        ],
        compiler_params=params(),
        name="edges",
    )(fetched, relations, slots)

    partial_grad = pl.pallas_call(
        return_kernel,
        out_shape=shape(entities.shape, f32),
        in_specs=[vmem] * 2,
        out_specs=vmem,
        scratch_shapes=[
            pltpu.VMEM((owners, message, LANES), f32),
            pltpu.VMEM((rows, wide), f32),
            pltpu.VMEM((NZ * LANES, wide), bf16),
            pltpu.VMEM((NZ * LANES, wide), bf16),
            dma,
            dma,
        ],
        compiler_params=params(collective_id=1, has_side_effects=True),
        name="give_back",
    )(out, asked)

    rel_summed = lax.psum(rel_grad, "rows")
    summed = lax.psum(partial_grad, "rel")
    new_entities, new_entity_state = adagrad_rows(entities, entity_state, summed)
    new_relations, new_relation_state = adagrad_dense(relations, relation_state, rel_summed)
    return (new_entities, new_entity_state, new_relations, new_relation_state)


def solution(mesh):
    placed = (
        P("rows", None),
        P("rows"),
        P("rel", None, None),
        P("rel", None, None),
        P(("rows", "rel"), None),
        P(("rows", "rel")),
        P(("rows", "rel"), None),
        P(("rows", "rel")),
        P(("rows", "rel")),
        P(("rows", "rel"), None),
        P(("rows", "rel")),
    )
    return jax.shard_map(
        per_device,
        mesh=mesh,
        in_specs=placed,
        out_specs=(P("rows", None), P("rows"), P("rel", None, None), P("rel", None, None)),
        check_vma=False,
    )
```

time: 770 us -> 627 us (0.81)
  Pallas kernels: 0 us -> 431 us
  waiting for transfers between devices: 535 us -> 154 us
  local copies, waits for them, and re-layouts: 91.7 us -> 15 us
  other arithmetic: 64.6 us -> 12.6 us
  starting transfers between devices: 31.1 us -> 0.26 us
  matrix products: 25.4 us -> 0 us
    pallas_call x0 -> x4, Pallas kernels: none -> 431 us  [the longest x1 199 us: per_device(): pl.pallas_call(fetch_kernel, out_shape=(shape((owners, message, LANES), f...]
    all_to_all x3 -> x0, waiting for transfers between devices: 416 us -> none  [the longest x1 206 us: per_device(): lax.all_to_all(outgoing.reshape(owners, slot_width, -1), 'rows', split_ax...]
    gather x6 -> x0, local copies, waits for them, and re-layouts: 39.4 us -> none  [the longest x1 17 us: per_device(): jnp.take(entities, requested, axis=0, mode='fill', fill_value=0.0)]
    scatter x6 -> x0, local copies, waits for them, and re-layouts: 35.6 us -> none  [the longest x3 27.7 us: per_device(): outgoing = jnp.zeros_like(fetched).at[head_slot].set(head_grad).at[tail_s...]
    psum x1, waiting for transfers between devices: 23 us -> 57.7 us  [per_device(): rel_summed = lax.psum(rel_grad, 'rows')]
    all_to_all x3 -> x0, starting transfers between devices: 31.1 us -> none  [the longest x1 13.2 us: per_device(): lax.all_to_all(wanted.reshape(owners, slot_width), 'rows', split_axis=0,...]
    scatter-add x1 -> x0, other arithmetic: 30.6 us -> none  [per_device(): partial_grad = jnp.zeros_like(entities).at[requested.reshape(-1)].add(ret...]
    dot_general x6 -> x0, matrix products: 25.4 us -> none  [the longest x1 5.03 us: edge_grads(): jnp.einsum('ed,ek,ef->kdf', head_vecs, member, proj_grad, precision=highest)]
  transfers between devices with their start and end apart: 5 -> 2, of which waited for: 5 -> 2; matrix products, arithmetic and copies ran while one was open for 6% -> 1% of each run, Pallas kernels for 0% -> 31%
where the time goes in v1:
time: 627 us; the launch traced here: 626 us
  Pallas kernels  431 us (69%)
  waiting for transfers between devices  154 us (25%)
  local copies, waits for them, and re-layouts  15 us (2%)
  between operations  14.1 us (2%)
  other arithmetic  12.6 us (2%)
    pallas_call x1, Pallas kernels, per_device(): pl.pallas_call(fetch_kernel, out_shape=(shape((owners, message, LANES), f...  199 us
    pallas_call x1, Pallas kernels, per_device(): pl.pallas_call(return_kernel, out_shape=shape(entities.shape, f32), in_sp...  191 us
    psum x1, waiting for transfers between devices, per_device(): summed = lax.psum(partial_grad, 'rel')  96 us
    psum x1, waiting for transfers between devices, per_device(): rel_summed = lax.psum(rel_grad, 'rows')  57.7 us
    pallas_call x1, Pallas kernels, per_device(): pl.pallas_call(edge_kernel, out_shape=(shape((owners, message, LANES), f3...  36.2 us
    unnamed x21, local copies, waits for them, and re-layouts  15 us
  transfers between devices with their start and end apart: 2, of which 2 were waited for; matrix products, arithmetic and copies ran while one was open for 1% of the time, Pallas kernels for 31%

profile of v1, /device:TPU:1, one launch (start us, length us, event | category | flops | bytes accessed | tf_op | source)
XLA Modules:
  0.0 626.2 jit_solution(17993189010987224625)
XLA Ops:
  7.2 0.0 all-reduce.5.cloned.1.call-start
  7.2 1.5 copy.15.hb
  8.7 1.5 copy.16.tb
  10.3 1.5 copy.17.nb
  11.8 0.0 copy-start.4
  11.8 0.0 copy-start.5
  11.8 0.0 copy-start.6
  11.8 0.0 copy-start.7
  11.8 5.0 copy.19.ent
  16.9 0.0 copy-done.4
  16.9 0.0 copy-done.5
  16.9 0.0 copy-done.6
  16.9 0.0 copy-done.7
  16.9 0.6 pad_add_fusion.rows
  17.5 4.0 route.1
  21.5 199.0 %fetch.1 = (f32[64,232,128]{2,1,0:T(8,128)}, f32[64,8,128]{2,1,0:T(8,128)}) custom-call(f32[64,8,128]{2,1,0:T(8,128)} %get-tuple-element.10.want, f32[2048,400]{1,0:T(8,128)} %copy.19.ent), custom_call_target="tpu_custom_call" | custom-call | tf_op jit(solution)/shard_map/fetch/pallas_call | solution.py:455
  220.5 36.2 %edges.1 = (f32[64,232,128]{2,1,0:T(8,128)}, f32[2,400,400]{2,1,0:T(8,128)}) custom-call(f32[64,232,128]{2,1,0:T(8,128)} %get-tuple-element.11.fetched, f32[2,400,400]{2,1,0:T(8,128)} %rel.1, f32[512,128]{1,0:T(8,128)} %get-tuple-element.12.slots), custom_call_target="tpu_custom_call" | custom-call | tf_op jit(solution)/shard_map/edges/pallas_call | solution.py:473
  256.8 0.0 all-reduce.5.cloned.1.call-update
  256.8 0.2 all-reduce.3.cloned.1.call-start
  257.0 191.4 %give_back.1 = f32[2048,400]{1,0:T(8,128)} custom-call(f32[64,232,128]{2,1,0:T(8,128)} %get-tuple-element.13.msgs, f32[64,8,128]{2,1,0:T(8,128)} %get-tuple-element.14.asked), custom_call_target="tpu_custom_call" | custom-call | tf_op jit(solution)/shard_map/give_back/pallas_call | solution.py:491
  448.4 0.0 copy-start.1
  448.4 0.0 copy-start.2
  448.4 0.0 all-reduce.3.cloned.1.call-update
  448.4 57.7 %all-reduce.5.cloned.1.call-done = f32[2,400,400]{2,1,0:T(8,128)} async-done(((f32[2,400,400]{2,1,0:T(8,128)}), f32[2,400,400]{2,1,0:T(8,128)}) %all-reduce.5.cloned.1.call-update) | async-done | bytes 1280016 | tf_op jit(solution)/shard_map/psum | solution.py:508
  506.1 0.0 copy-done.1
  506.1 0.0 copy-done.2
  506.1 3.8 multiply_subtract_fusion
  509.9 0.0 copy-start.3
  509.9 96.0 %all-reduce.3.cloned.1.call-done = f32[2048,400]{1,0:T(8,128)} async-done(((f32[2048,400]{1,0:T(8,128)}), f32[2048,400]{1,0:T(8,128)}) %all-reduce.3.cloned.1.call-update) | async-done | bytes 3276816 | tf_op jit(solution)/shard_map/psum | solution.py:509
  605.9 0.0 copy-start
  605.9 2.7 multiply_reduce_fusion
  608.6 0.0 copy-done.3
  608.6 0.6 fusion
  609.2 0.1 copy-done
  609.4 4.9 divide_subtract_fusion
  614.2 5.2 copy.20
Async XLA Ops:
  7.2 499.0 %all-reduce.5.cloned.1.call-start = ((), (), s32[]{:S(2)}) async-start(), calls=%async_computation.1 | async-start | bytes 3276800 | tf_op jit(solution)/shard_map/psum | solution.py:508
  11.8 5.0 copy-start.4
  11.8 5.0 copy-start.5
  11.8 5.0 copy-start.6
  11.8 5.0 copy-start.7
  256.8 349.1 %all-reduce.3.cloned.1.call-start = ((), (), s32[]{:S(2)}) async-start(), calls=%async_computation | async-start | bytes 8388608 | tf_op jit(solution)/shard_map/psum | solution.py:509
  448.4 57.7 %copy-start.1 = (f32[2,400,400]{2,1,0:T(8,128)S(1)}, f32[2,400,400]{2,1,0:T(8,128)}, u32[]{:S(2)}) copy-start(f32[2,400,400]{2,1,0:T(8,128)} %rel.1) | copy-start | bytes 3840004
  448.4 57.7 %copy-start.2 = (f32[2,400,400]{2,1,0:T(8,128)S(1)}, f32[2,400,400]{2,1,0:T(8,128)}, u32[]{:S(2)}) copy-start(f32[2,400,400]{2,1,0:T(8,128)} %param.14) | copy-start | bytes 3840004
  509.9 98.7 %copy-start.3 = (f32[2048]{0:T(1024)S(1)}, f32[2048]{0:T(1024)}, u32[]{:S(2)}) copy-start(f32[2048]{0:T(1024)} %param.12) | copy-start | bytes 24580
  605.9 3.4 copy-start
Sparse Core Ops, SparseCore 0:
  256.9 249.1 all-reduce.4
  508.5 97.3 all-reduce.2

commit v2 on v1

--- a/solution.py
+++ b/solution.py
@@ -51,30 +51,31 @@
     )
 
 
-def route_kernel(cap, hb, tb, nb, rows, want_ref, slot_ref):
-    n = hb.shape[0]
+def route_kernel(cap, hb, tb, nb, hr, tr, nr, rel_slot, want_ref, slot_ref):
+    n = hb.shape[1]
     owners = want_ref.shape[0]
     before = (iota((n, n), 1) < iota((n, n), 0)).astype(bf16)
     lists = jnp.zeros((owners, LANES), f32)
     slots = jnp.zeros((n, LANES), f32)
     lane = iota((n, LANES), 1).astype(f32)
-    for s, ref in enumerate((hb, tb, nb)):
-        block = ref[...].astype(f32)
+    for s, (ref, row) in enumerate(((hb, hr), (tb, tr), (nb, nr))):
+        block_row = ref[...].astype(f32)
+        block = as_column(block_row, n)
         member = lane == block
         earlier = mm(before, member.astype(bf16))
         pos = jnp.sum(jnp.where(member, earlier, 0.0), axis=1, keepdims=True)
         slots = jnp.where(lane == s, block * cap + pos, slots)
-        value = as_column(rows[s : s + 1, :].astype(f32), n) + 1.0
+        value = as_column(row[...].astype(f32), n) + 1.0
         high = jnp.floor(value * (1.0 / 64.0))
         low = value - 64.0 * high
         at = lane == pos + float(cap * s)
-        to_owner = (iota((owners, n), 0).astype(f32) == as_row(block, n)).astype(bf16)
+        to_owner = (iota((owners, n), 0).astype(f32) == block_row).astype(bf16)
         lists = (
             lists
             + 64.0 * mm(to_owner, jnp.where(at, high, 0.0).astype(bf16))
             + mm(to_owner, jnp.where(at, low, 0.0).astype(bf16))
         )
-    slots = jnp.where(lane == 3, as_column(rows[3:4, :].astype(f32), n), slots)
+    slots = jnp.where(lane == 3, as_column(rel_slot[...].astype(f32), n), slots)
     want_ref[...] = jnp.broadcast_to((lists - 1.0)[:, None, :], want_ref.shape)
     slot_ref[...] = slots
 
@@ -88,8 +89,10 @@
     return ((z + NZ - dz) % NZ) * nyc + (yc + 2 * nyc - b - j % nyc) % nyc
 
 
-def meet_all(nyc):
+def meet_all(nyc, beside=()):
     barrier = pltpu.get_barrier_semaphore()
+    for p in beside:
+        pl.semaphore_signal(barrier, inc=1, device_id={"rel": p}, device_id_type=MESH)
 
     def greet(b, carry):
         for j in range(NZ):
@@ -105,7 +108,7 @@
         return carry
 
     lax.fori_loop(0, nyc, greet, 0)
-    pl.semaphore_wait(barrier, NZ * nyc - 1)
+    pl.semaphore_wait(barrier, NZ * nyc - 1 + len(beside))
 
 
 def for_others(nyc, sign, body):
@@ -133,7 +136,7 @@
     me = lax.axis_index("rows")
     owners = want.shape[0]
     nyc = owners // NZ
-    rows, width = ent.shape
+    width, rows = ent.shape
     full = width // LANES * LANES
     slots = 72
     meet_all(nyc)
@@ -146,14 +149,10 @@
 
     def cut(i, carry):
         at = pl.ds(pl.multiple_of(i * 256, 256), 256)
-        h, l = split(ent[at, :full])
-        hi[at, :full] = h
-        lo[at, :full] = l
-        hi[at, full:] = jnp.zeros((256, LANES), bf16)
-        lo[at, full:] = jnp.zeros((256, LANES), bf16)
-        h, l = split(ent[at, full:])
-        hi[at, full:width] = h
-        lo[at, full:width] = l
+        for c in range(full // LANES + 1):
+            h, l = split(plane_of(ent, c, at))
+            hi[at, c * LANES : (c + 1) * LANES] = h
+            lo[at, c * LANES : (c + 1) * LANES] = l
         return carry
 
     lax.fori_loop(0, rows // 256, cut, 0)
@@ -194,27 +193,43 @@
     for_others(nyc, 1, finish)
 
 
+def plane_of(turned, c, at):
+    part = turned[c * LANES : min((c + 1) * LANES, turned.shape[0]), at]
+    if part.shape[0] < LANES:
+        gap = jnp.zeros((LANES - part.shape[0], part.shape[1]), part.dtype)
+        part = jnp.concatenate([part, gap], axis=0)
+    return part.T
+
+
+def pack_tail(tail):
+    packed = tail[0:8]
+    for g in range(1, 8):
+        packed = packed + pltpu.roll(tail[8 * g : 8 * g + 8], 16 * g, 1)
+    return packed
+
+
+def open_tail(packed):
+    low = iota((8, LANES), 1) < 16
+    parts = [jnp.where(low, packed, 0.0)]
+    for g in range(1, 8):
+        parts.append(jnp.where(low, pltpu.roll(packed, LANES - 16 * g, 1), 0.0))
+    return jnp.concatenate(parts, axis=0)
+
+
 def pack(ref, p, block):
     slots = block.shape[0]
     planes = block.shape[1] // LANES - 1
     for c in range(planes):
         ref[p, c * slots : (c + 1) * slots, :] = block[:, c * LANES : (c + 1) * LANES]
     tail = block[:, planes * LANES :]
-    packed = tail[0:8]
-    for g in range(1, 8):
-        packed = packed + pltpu.roll(tail[8 * g : 8 * g + 8], 16 * g, 1)
-    ref[p, planes * slots : planes * slots + 8, :] = packed
+    ref[p, planes * slots : planes * slots + 8, :] = pack_tail(tail)
     ref[p, planes * slots + 8 : planes * slots + 16, :] = tail[64:72]
 
 
 def unpack_tail(ref, p, base):
-    packed = ref[p, base : base + 8, :]
-    low = iota((8, LANES), 1) < 16
-    parts = [jnp.where(low, packed, 0.0)]
-    for g in range(1, 8):
-        parts.append(jnp.where(low, pltpu.roll(packed, LANES - 16 * g, 1), 0.0))
-    parts.append(ref[p, base + 8 : base + 16, :])
-    return jnp.concatenate(parts, axis=0)
+    return jnp.concatenate(
+        [open_tail(ref[p, base : base + 8, :]), ref[p, base + 8 : base + 16, :]], axis=0
+    )
 
 
 def edge_kernel(
@@ -343,15 +358,19 @@
         lax.fori_loop(0, owners // 8, spread, 0)
 
 
-def return_kernel(msgs, asked, total, back, acc, xh, xl, send, recv):
+def return_kernel(
+    msgs, asked, ent, state, out, new_state, back, acc, xh, xl, part, land, done, send, recv, xsend, xrecv
+):
     me = lax.axis_index("rows")
     owners = msgs.shape[0]
     nyc = owners // NZ
-    rows, width = total.shape
+    width, rows = ent.shape
     full = width // LANES * LANES
     slots = 72
     planes = full // LANES
-    meet_all(nyc)
+    here = lax.axis_index("rel")
+    right, left, across = (here + 1) % 4, (here + 3) % 4, (here + 2) % 4
+    meet_all(nyc, (right, left))
 
     def copy(p, slot):
         return remote(msgs.at[p], back.at[slot], send.at[p], recv.at[slot], p)
@@ -398,18 +417,122 @@
 
     lax.fori_loop(0, nyc, take, 0)
 
-    def store(i, carry):
-        at = pl.ds(pl.multiple_of(i * 256, 256), 256)
-        total[at, :] = acc[at, :][:, :width]
-        return carry
-
-    lax.fori_loop(0, rows // 256, store, 0)
+    half = rows // 8
+    tails = planes * half
+    states = tails + half // 8
+
+    def lay(i, carry):
+        at = pl.ds(pl.multiple_of(i * half, half), half)
+        for c in range(planes):
+            part[i, c * half : (c + 1) * half, :] = acc[at, c * LANES : (c + 1) * LANES]
+        tail = acc[at, full:]
+        for u in range(half // 64):
+            part[i, tails + 8 * u : tails + 8 * u + 8, :] = pack_tail(tail[64 * u : 64 * u + 64])
+        part[i, states : states + 8, :] = jnp.zeros((8, LANES), f32)
+        return carry
+
+    lax.fori_loop(0, 8, lay, 0)
+
+    def xcopy(k, src, dst, to):
+        return pltpu.make_async_remote_copy(
+            src_ref=src,
+            dst_ref=dst,
+            send_sem=xsend.at[k],
+            recv_sem=xrecv.at[k],
+            device_id={"rel": to},
+            device_id_type=MESH,
+        )
+
+    sums = [
+        xcopy(0, part.at[2 * across], land.at[0], left),
+        xcopy(1, part.at[2 * across + 1], land.at[1], right),
+        xcopy(2, part.at[2 * left + 1], land.at[2], left),
+        xcopy(3, part.at[2 * right], land.at[3], right),
+        xcopy(4, part.at[2 * left], land.at[4], left),
+        xcopy(5, part.at[2 * right + 1], land.at[5], right),
+    ]
+    for k in range(4):
+        sums[k].start()
+    sums[0].wait_recv()
+    part[2 * left] = part[2 * left] + land[0]
+    sums[4].start()
+    sums[1].wait_recv()
+    part[2 * right + 1] = part[2 * right + 1] + land[1]
+    sums[5].start()
+
+    def update(h, first, second):
+        i = 2 * here + h
+        done[i, states : states + 8, :] = jnp.zeros((8, LANES), f32)
+        for u in range(half // LANES):
+
+            def summed(a, n):
+                return part[i, a : a + n, :] + land[first, a : a + n, :] + land[second, a : a + n, :]
+
+            at = pl.ds(pl.multiple_of(i * half + u * LANES, LANES), LANES)
+            grad = [summed(c * half + u * LANES, LANES) for c in range(planes)]
+            packed = summed(tails + 16 * u, 16)
+            grad.append(jnp.concatenate([open_tail(packed[0:8]), open_tail(packed[8:16])], axis=0))
+            squares = sum(g * g for g in grad)
+            before = as_column(state[pl.ds(i * (half // LANES) + u, 1), :], LANES)
+            after = before + jnp.sum(squares, axis=1, keepdims=True) * (1.0 / width)
+            rate = entity_rate / jnp.sqrt(after)
+            for c, g in enumerate(grad):
+                new = plane_of(ent, c, at) - rate * g
+                if c < planes:
+                    done[i, c * half + u * LANES : c * half + (u + 1) * LANES, :] = new
+                else:
+                    for w in range(2):
+                        k = tails + 16 * u + 8 * w
+                        done[i, k : k + 8, :] = pack_tail(new[64 * w : 64 * w + 64])
+            done[i, states + u : states + u + 1, :] = as_row(after, LANES)
+        return i
+
+    def spread(k, i, to):
+        return xcopy(k, done.at[i], done.at[i], to)
+
+    def write(i):
+        at = pl.ds(pl.multiple_of(i * half, half), half)
+        for c in range(planes):
+            out[c * LANES : (c + 1) * LANES, at] = done[i, c * half : (c + 1) * half, :].T
+        tail = jnp.concatenate(
+            [open_tail(done[i, tails + 8 * u : tails + 8 * u + 8, :]) for u in range(half // 64)], axis=0
+        )
+        out[full:width, at] = tail.T[0 : width - full]
+        new_state[i] = done[i, states : states + 8, :]
+
+    sums[3].wait_recv()
+    sums[4].wait_recv()
+    mine = update(0, 3, 4)
+    spread(6, mine, left).start()
+    spread(7, mine, right).start()
+    sums[2].wait_recv()
+    sums[5].wait_recv()
+    mine = update(1, 2, 5)
+    spread(8, mine, left).start()
+    spread(9, mine, right).start()
+    write(2 * here)
+    write(2 * here + 1)
+    spread(7, 2 * left, right).wait_recv()
+    spread(10, 2 * left, right).start()
+    write(2 * left)
+    spread(8, 2 * right + 1, left).wait_recv()
+    spread(11, 2 * right + 1, left).start()
+    write(2 * right + 1)
+    spread(6, 2 * right, left).wait_recv()
+    write(2 * right)
+    spread(9, 2 * left + 1, right).wait_recv()
+    write(2 * left + 1)
+    spread(10, 2 * across, right).wait_recv()
+    write(2 * across)
+    spread(11, 2 * across + 1, left).wait_recv()
+    write(2 * across + 1)
+    for k in range(6):
+        sums[k].wait_send()
+    for k, i in ((6, 2 * here), (7, 2 * here), (8, 2 * here + 1), (9, 2 * here + 1)):
+        spread(k, i, left).wait_send()
+    spread(10, 2 * left, right).wait_send()
+    spread(11, 2 * right + 1, left).wait_send()
     for_others(nyc, 1, lambda p: copy(p, p).wait_send())
-
-
-def adagrad_rows(row_block, accum, gradient):
-    updated = accum + jnp.mean(gradient * gradient, axis=1)
-    return (row_block - entity_rate * gradient / jnp.sqrt(updated)[:, None], updated)
 
 
 def adagrad_dense(params, accum, gradient):
@@ -442,15 +565,18 @@
     params = functools.partial(pltpu.CompilerParams, vmem_limit_bytes=VMEM_LIMIT)
     dma = pltpu.SemaphoreType.DMA((owners,))
 
-    rows_in = jnp.stack([head_row, tail_row, neg_row, rel_slot])
+    lanes = [
+        a.reshape(1, edges)
+        for a in (head_block, tail_block, neg_block, head_row, tail_row, neg_row, rel_slot)
+    ]
     want, slots = pl.pallas_call(
         functools.partial(route_kernel, cap),
         out_shape=(shape((owners, 8, LANES), f32), shape((edges, LANES), f32)),
-        in_specs=[vmem] * 4,
+        in_specs=[vmem] * 7,
         out_specs=(vmem, vmem),
         compiler_params=params(),
         name="route",
-    )(head_block, tail_block, neg_block, rows_in)
+    )(*lanes)
 
     fetched, asked = pl.pallas_call(
         fetch_kernel,
@@ -468,7 +594,7 @@
         ],
         compiler_params=params(collective_id=0, has_side_effects=True),
         name="fetch",
-    )(want, entities)
+    )(want, entities.T)
 
     out, rel_grad = pl.pallas_call(
         edge_kernel,
@@ -488,26 +614,32 @@
         name="edges",
     )(fetched, relations, slots)
 
-    partial_grad = pl.pallas_call(
+    rel_summed = lax.psum(rel_grad, "rows")
+    block = full // LANES * (rows // 8) + rows // 64 + 8
+    turned, states = pl.pallas_call(
         return_kernel,
-        out_shape=shape(entities.shape, f32),
-        in_specs=[vmem] * 2,
-        out_specs=vmem,
+        out_shape=(shape((width, rows), f32), shape((8, 8, LANES), f32)),
+        in_specs=[vmem] * 4,
+        out_specs=(vmem, vmem),
         scratch_shapes=[
             pltpu.VMEM((owners, message, LANES), f32),
             pltpu.VMEM((rows, wide), f32),
             pltpu.VMEM((NZ * LANES, wide), bf16),
             pltpu.VMEM((NZ * LANES, wide), bf16),
+            pltpu.VMEM((8, block, LANES), f32),
+            pltpu.VMEM((6, block, LANES), f32),
+            pltpu.VMEM((8, block, LANES), f32),
             dma,
             dma,
+            pltpu.SemaphoreType.DMA((12,)),
+            pltpu.SemaphoreType.DMA((12,)),
         ],
         compiler_params=params(collective_id=1, has_side_effects=True),
         name="give_back",
-    )(out, asked)
-
-    rel_summed = lax.psum(rel_grad, "rows")
-    summed = lax.psum(partial_grad, "rel")
-    new_entities, new_entity_state = adagrad_rows(entities, entity_state, summed)
+    )(out, asked, entities.T, entity_state.reshape(rows // LANES, LANES))
+
+    new_entities = turned.T
+    new_entity_state = states[:, : rows // 8 // LANES].reshape(rows)
     new_relations, new_relation_state = adagrad_dense(relations, relation_state, rel_summed)
     return (new_entities, new_entity_state, new_relations, new_relation_state)
 

time: 627 us -> 514 us (0.82)
  waiting for transfers between devices: 154 us -> 8.04 us
  Pallas kernels: 431 us -> 483 us
  local copies, waits for them, and re-layouts: 15 us -> 3.08 us
  other arithmetic: 12.6 us -> 3.94 us
    psum x1 -> x0, waiting for transfers between devices: 96 us -> none  [per_device(): summed = lax.psum(partial_grad, 'rel')]
    pallas_call x1, Pallas kernels: 191 us -> 246 us  [per_device(): pl.pallas_call(return_kernel, out_shape=(shape((width, rows), f32), shape...]
    psum x1, waiting for transfers between devices: 57.7 us -> 8.02 us  [per_device(): rel_summed = lax.psum(rel_grad, 'rows')]
    unnamed x21 -> x7, local copies, waits for them, and re-layouts: 15 us -> 1.72 us
  transfers between devices with their start and end apart: 2 -> 1, of which waited for: 2 -> 1; matrix products, arithmetic and copies ran while one was open for 1% -> 0% of each run, Pallas kernels for 31% -> 48%
where the time goes in v2:
time: 514 us; the launch traced here: 512 us
  Pallas kernels  483 us (94%)
  between operations  14.1 us (3%)
  waiting for transfers between devices  8.04 us (2%)
    pallas_call x1, Pallas kernels, per_device(): pl.pallas_call(return_kernel, out_shape=(shape((width, rows), f32), shape...  246 us
    pallas_call x1, Pallas kernels, per_device(): pl.pallas_call(fetch_kernel, out_shape=(shape((owners, message, LANES), f...  198 us
    pallas_call x1, Pallas kernels, per_device(): pl.pallas_call(edge_kernel, out_shape=(shape((owners, message, LANES), f3...  36.2 us
  transfers between devices with their start and end apart: 1, of which 1 were waited for; matrix products, arithmetic and copies ran while one was open for 0% of the time, Pallas kernels for 48%

profile of v2, /device:TPU:1, one launch (start us, length us, event | category | flops | bytes accessed | tf_op | source)
XLA Modules:
  0.0 512.5 jit_solution(5473920004804702291)
XLA Ops:
  7.2 0.0 all-reduce.2.cloned.1.call-start
  7.2 3.0 route.1
  10.2 198.3 %fetch.1 = (f32[64,232,128]{2,1,0:T(8,128)}, f32[64,8,128]{2,1,0:T(8,128)}) custom-call(f32[64,8,128]{2,1,0:T(8,128)} %get-tuple-element.12.want, f32[400,2048]{1,0:T(8,128)} %bitcast.11), custom_call_target="tpu_custom_call" | custom-call | tf_op jit(solution)/shard_map/fetch/pallas_call | solution.py:581
  208.5 36.2 %edges.1 = (f32[64,232,128]{2,1,0:T(8,128)}, f32[2,400,400]{2,1,0:T(8,128)}) custom-call(f32[64,232,128]{2,1,0:T(8,128)} %get-tuple-element.13.fetched, f32[2,400,400]{2,1,0:T(8,128)} %rel.1, f32[512,128]{1,0:T(8,128)} %get-tuple-element.14.slots), custom_call_target="tpu_custom_call" | custom-call | tf_op jit(solution)/shard_map/edges/pallas_call | solution.py:599
  244.7 0.0 all-reduce.2.cloned.1.call-update
  244.7 0.0 copy-start
  244.8 0.0 copy-start.2
  244.8 245.8 %give_back.1 = (f32[400,2048]{1,0:T(8,128)}, f32[8,8,128]{2,1,0:T(8,128)}) custom-call(f32[64,232,128]{2,1,0:T(8,128)} %get-tuple-element.15.msgs, f32[64,8,128]{2,1,0:T(8,128)} %get-tuple-element.16.asked, f32[400,2048]{1,0:T(8,128)} %bitcast.12, f32[16,128]{1,0:T(8,128)} %bitcast.14), custom_call_target="tpu_custom_call" | custom-call | tf_op jit(solution)/shard_map/give_back/pallas_call | solution.py:619
  490.6 1.4 slice.3
  492.0 8.0 %all-reduce.2.cloned.1.call-done = f32[2,400,400]{2,1,0:T(8,128)} async-done(((f32[2,400,400]{2,1,0:T(8,128)}), f32[2,400,400]{2,1,0:T(8,128)}) %all-reduce.2.cloned.1.call-update) | async-done | bytes 1280016 | tf_op jit(solution)/shard_map/psum | solution.py:617
  500.0 0.0 copy-done
  500.0 0.0 copy-done.2
  500.0 0.0 copy-start.1
  500.0 3.9 multiply_subtract_fusion
  503.9 0.0 copy-done.1
  503.9 1.7 copy.17
Async XLA Ops:
  7.2 492.8 %all-reduce.2.cloned.1.call-start = ((), (), s32[]{:S(2)}) async-start(), calls=%async_computation | async-start | bytes 3276800 | tf_op jit(solution)/shard_map/psum | solution.py:617
  244.7 255.2 %copy-start = (f32[2,400,400]{2,1,0:T(8,128)S(1)}, f32[2,400,400]{2,1,0:T(8,128)}, u32[]{:S(2)}) copy-start(f32[2,400,400]{2,1,0:T(8,128)} %rel.1) | copy-start | bytes 3840004
  244.8 255.2 %copy-start.2 = (f32[2,400,400]{2,1,0:T(8,128)S(1)}, f32[2,400,400]{2,1,0:T(8,128)}, u32[]{:S(2)}) copy-start(f32[2,400,400]{2,1,0:T(8,128)} %param.14) | copy-start | bytes 3840004
  500.0 3.9 copy-start.1
Sparse Core Ops, SparseCore 0:
  244.9 255.0 all-reduce.1
